TPU v7x, 32 devices: a whole 2x2x4 slice. The times are simulated.
32 devices in a mesh: mem: 4 (over y, x), brick: 8 (over z, core).
Axes of the slice: x: 2, y: 2, z: 4, core: 2. Of those that a mesh axis runs over, the one named last changes fastest.
Arguments:
- members: float32 [128, 131072], P('mem', 'brick'), may hold values from -6 to 6
- predicted: float32 [128, 40, 1024], P('brick', None, 'mem'), may hold values from -6 to 6
- perturbation: float32 [128, 40, 1024], P('brick', None, 'mem'), may hold values from -6 to 6
- observed: float32 [40, 1024], P(None, ('mem', 'brick')), may hold values from -6 to 6
- noise_std: float32 [40, 1024], P(None, ('mem', 'brick')), may hold values from 0.3 to 3
- taper_weights: bfloat16 [1024, 512], P(('mem', 'brick')), may hold values from 0.099609375 to 1
- foot_brick: int32 [1024, 1], P(('mem', 'brick')), may hold values from 0 to 7; in each aligned block of 32 rows (0 to 31, 32 to 63, ...) at most 8 rows name the same one
- foot_tiles: int32 [1024, 4], P(('mem', 'brick')), may hold values from 0 to 127
Outputs:
- updated: float32 [128, 131072], P('mem', 'brick')
Inputs may be any that keep to these rules, and one draw needn't show every extreme that they name: `foot_brick`: among the 32 soundings of one owner (aligned blocks of rows) at most 8 have their footprint in one brick, and some brick receives exactly 8 from some owner in every draw. `foot_tiles`: tile numbers inside the sounding's brick.
All inputs are finite; a program needn't handle non-finite values.
Results may differ from a plain program's by a relative error of at most 0.012.
Values may be sent and summed in bfloat16 or wider, within the bound.
A program may use at most 64 MiB of HBM per device.

v0:
```python
import jax
import jax.numpy as jnp
from jax import lax
from jax.experimental import pallas as pl
from jax.experimental.pallas import tpu as pltpu
from jax.sharding import PartitionSpec as P

GROUP = 4
PIECES = 4
HIGH = lax.Precision.HIGHEST


def owner_kernel(
    index_ref,
    pair_ref,
    obs_ref,
    std_ref,
    taper_ref,
    out_ref,
    data,
    anom,
    misf,
    cov,
    work,
    inv,
    stage_a,
    stage_g,
    landed_a,
    landed_g,
    spread,
    p_send,
    p_recv,
    a_send,
    a_recv,
    g_send,
    g_recv,
    m_send,
    m_recv,
):
    mem_count, bricks, out_rows, _ = out_ref.shape
    _, soundings, part, lanes = pair_ref.shape
    ensemble = bricks * part
    gates = obs_ref.shape[1]
    tail = taper_ref.shape[1]
    cap = index_ref.shape[0] // bricks
    block = (out_rows - tail) // cap
    held_rows = cap * gates
    at_m = lax.axis_index("mem")
    at_b = lax.axis_index("brick")
    mesh_ids = pl.DeviceIdType.MESH

    barrier = pltpu.get_barrier_semaphore()
    for d in range(1, bricks):
        pl.semaphore_signal(
            barrier, inc=1, device_id=(at_m, lax.rem(at_b + d, bricks)), device_id_type=mesh_ids
        )
    for e in range(1, mem_count):
        pl.semaphore_signal(
            barrier, inc=1, device_id=(lax.rem(at_m + e, mem_count), at_b), device_id_type=mesh_ids
        )
    pl.semaphore_wait(barrier, bricks + mem_count - 2)

    def along_brick(d, source, target, send_sem, recv_sem):
        there = lax.rem(at_b + d, bricks)
        return pltpu.make_async_remote_copy(
            src_ref=source.at[there],
            dst_ref=target.at[at_b],
            send_sem=send_sem.at[d],
            recv_sem=recv_sem.at[d],
            device_id=(at_m, there),
            device_id_type=mesh_ids,
        )

    piece = soundings // PIECES

    def send_pair(d, h):
        there = lax.rem(at_b + d, bricks)
        return pltpu.make_async_remote_copy(
            src_ref=pair_ref.at[there, pl.ds(h * piece, piece)],
            dst_ref=data.at[at_b, pl.ds(h * piece, piece)],
            send_sem=p_send.at[h * bricks + d],
            recv_sem=p_recv.at[h * bricks + d],
            device_id=(at_m, there),
            device_id_type=mesh_ids,
        )

    def send_anomaly(d):
        return along_brick(d, stage_a, landed_a, a_send, a_recv)

    def send_gain(d):
        return along_brick(d, stage_g, landed_g, g_send, g_recv)

    def to_member(d, e):
        source = lax.rem(at_b - d + bricks, bricks)
        there = lax.rem(at_m + e, mem_count)
        return pltpu.make_async_remote_copy(
            src_ref=spread.at[source, there],
            dst_ref=out_ref.at[at_m, source],
            send_sem=m_send.at[d * mem_count + e],
            recv_sem=m_recv.at[d * mem_count + e],
            device_id=(there, at_b),
            device_id_type=mesh_ids,
        )

    def each_peer(step):
        def turn(d, carry):
            step(d)
            return carry

        lax.fori_loop(1, bricks, turn, 0)

    for h in range(PIECES):
        each_peer(lambda d: send_pair(d, h).start())
    data[at_b] = pair_ref[at_b]

    row = lax.broadcasted_iota(jnp.int32, (gates, gates), 0)
    column = lax.broadcasted_iota(jnp.int32, (gates, gates), 1)

    def prepare(s, carry):
        turned = data[:, s].astype(jnp.float32).reshape(ensemble, lanes).T
        pred = turned[:gates]
        pert = turned[gates : 2 * gates]
        std = std_ref[s]
        anomaly = pred - jnp.sum(pred, axis=1, keepdims=True) / ensemble
        misf[s] = obs_ref[s] + std * pert - pred
        anom[s] = anomaly
        total = lax.dot_general(
            anomaly,
            anomaly,
            (((1,), (1,)), ((), ())),
            precision=HIGH,
            preferred_element_type=jnp.float32,
        ) / (ensemble - 1.0)
        cov[s] = total + jnp.where(row == column, std * std, 0.0)
        return carry

    for h in range(PIECES):
        each_peer(lambda d: send_pair(d, h).wait())
        lax.fori_loop(h * piece, (h + 1) * piece, prepare, 0, unroll=4)

    def pack(values, ref, place, there):
        for r in range(0, cap, 2):
            first = values[index_ref[there * cap + r]]
            second = values[index_ref[there * cap + r + 1]]
            both = jnp.concatenate([first, second], axis=0).astype(jnp.bfloat16)
            ref[place, pl.ds(r * gates, 2 * gates), :] = both

    def post_anomaly(d):
        there = lax.rem(at_b + d, bricks)
        pack(anom, stage_a, there, there)
        stage_a[there, pl.ds(held_rows, tail), :] = taper_ref[there]
        send_anomaly(d).start()

    each_peer(post_anomaly)
    pack(anom, landed_a, at_b, at_b)
    landed_a[at_b, pl.ds(held_rows, tail), :] = taper_ref[at_b]

    for i in range(gates):
        work[i] = cov[:, i, :].T

    place = lax.broadcasted_iota(jnp.int32, (gates, soundings), 0)

    def sweep(k, carry):
        scale = 1.0 / work[k, pl.ds(k, 1), :]
        pivot = work[k]
        scaled = jnp.where(place == k, scale, pivot * scale)
        kept = jnp.where(place == k, 0.0, 1.0)
        for i in range(gates):
            coef = work[i, pl.ds(k, 1), :]
            work[i] = work[i] * kept - coef * scaled
        work[k] = scaled
        return carry

    lax.fori_loop(0, gates, sweep, 0)

    for i in range(gates):
        inv[:, i, :] = work[i].T

    def finish(s, carry):
        misf[s] = lax.dot_general(
            inv[s],
            misf[s],
            (((1,), (0,)), ((), ())),
            precision=HIGH,
            preferred_element_type=jnp.float32,
        ) / (ensemble - 1.0)
        return carry

    lax.fori_loop(0, soundings, finish, 0, unroll=4)

    def post_gain(d):
        there = lax.rem(at_b + d, bricks)
        pack(misf, stage_g, there, there)
        send_gain(d).start()

    each_peer(post_gain)
    pack(misf, landed_g, at_b, at_b)

    def weigh(d):
        source = lax.rem(at_b - d + bricks, bricks)
        for r in range(0, cap, 2):
            gains = landed_g[source, pl.ds(r * gates, 2 * gates), :].astype(jnp.float32)
            anomalies = landed_a[source, pl.ds(r * gates, 2 * gates), :].astype(jnp.float32)
            for h in range(2):
                weight = jnp.dot(
                    gains[h * gates : (h + 1) * gates].T.astype(jnp.bfloat16),
                    anomalies[h * gates : (h + 1) * gates].astype(jnp.bfloat16),
                    preferred_element_type=jnp.float32,
                ).astype(jnp.bfloat16)
                for m in range(mem_count):
                    spread[source, m, pl.ds((r + h) * block, block), :] = weight[
                        m * block : (m + 1) * block
                    ]
        tapers = landed_a[source, pl.ds(held_rows, tail), :]
        for m in range(mem_count):
            spread[source, m, pl.ds(cap * block, tail), :] = tapers
        for e in range(1, mem_count):
            to_member(d, e).start()
        out_ref[at_m, source] = spread[source, at_m]

    weigh(0)

    def take(d):
        send_anomaly(d).wait_recv()
        send_gain(d).wait_recv()
        weigh(d)

    each_peer(take)

    def sent(d):
        send_anomaly(d).wait_send()
        send_gain(d).wait_send()

    each_peer(sent)

    def settle(d, carry):
        for e in range(1, mem_count):
            to_member(d, e).wait()
        return carry

    lax.fori_loop(0, bricks, settle, 0)


def update_kernel(
    count_ref, slot_ref, tile_ref, recv_ref, model_ref, members_ref, out_ref, tapers
):
    foot = tile_ref.shape[0]
    block = members_ref.shape[0]
    cap = slot_ref.shape[0] // recv_ref.shape[0]
    total = count_ref[0]
    out_ref[...] = members_ref[...]
    tapers[...] = recv_ref[:, cap * block : cap * (block + foot), :].astype(jnp.float32)

    def turn(step, carry):
        results = []
        for u in range(GROUP):
            at = step * GROUP + u
            owner = slot_ref[at] // cap
            rank = slot_ref[at] % cap
            weight = recv_ref[owner, pl.ds(pl.multiple_of(rank * block, block), block), :]
            used = at < total
            starts = [pl.multiple_of(tile_ref[c, at] * 128, 128) for c in range(foot)]
            cells = jnp.concatenate([model_ref[:, pl.ds(start, 128)] for start in starts], axis=1)
            part = jnp.dot(weight, cells, preferred_element_type=jnp.float32)
            for c, start in enumerate(starts):
                taper = tapers[owner, pl.ds(rank * foot + c, 1), :]
                scaled = part[:, c * 128 : (c + 1) * 128] * taper
                results.append((start, jnp.where(used, scaled, 0.0)))
        for start, scaled in results:
            out_ref[:, pl.ds(start, 128)] += scaled
        return carry

    lax.fori_loop(0, (total + GROUP - 1) // GROUP, turn, 0)


def body(
    members, predicted, perturbation, observed, noise_std, taper_weights, foot_brick, foot_tiles
):
    mem_count = lax.axis_size("mem")
    brick_count = lax.axis_size("brick")
    part, gates, wide = predicted.shape
    ensemble = part * brick_count
    local = wide // brick_count
    block = ensemble // mem_count
    foot = foot_tiles.shape[1]
    foot_length = taper_weights.shape[1]
    devices = mem_count * brick_count
    cap = max(2, 2 * local // brick_count)
    slots = devices * cap
    vmem = pltpu.CompilerParams(vmem_limit_bytes=48 * 1024 * 1024)
    in_vmem = pl.BlockSpec(memory_space=pltpu.VMEM)
    in_smem = pl.BlockSpec(memory_space=pltpu.SMEM)

    model_all = lax.all_gather(members.astype(jnp.bfloat16), "mem", axis=0, tiled=True)

    pair = jnp.concatenate([predicted, perturbation], axis=1).astype(jnp.bfloat16)
    pair = jnp.transpose(pair, (2, 0, 1))
    pair = jnp.pad(pair, ((0, 0), (0, 0), (0, 128 - 2 * gates)))
    pair = pair.reshape(brick_count, local, part, 128)
    destination = foot_brick[:, 0]
    order = jnp.arange(local)
    before = order[None, :] < order[:, None]
    rank = jnp.sum(
        ((destination[:, None] == destination[None, :]) & before).astype(jnp.int32), axis=1
    )
    slot_of = destination * cap + rank
    hot = slot_of[None, :] == jnp.arange(brick_count * cap, dtype=jnp.int32)[:, None]
    index = jnp.sum(jnp.where(hot, order[None, :], 0), axis=1)
    numbers = jnp.concatenate([foot_tiles, jnp.ones((local, 1), jnp.int32)], axis=1)
    numbers = jnp.pad(numbers.astype(jnp.bfloat16), ((0, 0), (0, 127 - foot)))
    extra = jnp.concatenate([taper_weights, numbers], axis=1)
    extra = jnp.dot(hot.astype(jnp.bfloat16), extra, preferred_element_type=jnp.float32)
    extra = extra.astype(jnp.bfloat16)
    taper_slots = extra[:, :foot_length].reshape(brick_count, cap * foot, 128)
    number_slots = extra[:, foot_length:].reshape(brick_count, cap, 128)
    tail = -(-cap * (foot + 1) // 16) * 16
    taper_slots = jnp.concatenate([taper_slots, number_slots], axis=1)
    taper_slots = jnp.pad(taper_slots, ((0, 0), (0, tail - cap * (foot + 1)), (0, 0)))

    out_rows = cap * block + tail
    recv = pl.pallas_call(
        owner_kernel,
        out_shape=jax.ShapeDtypeStruct((mem_count, brick_count, out_rows, 128), jnp.bfloat16),
        in_specs=[in_smem] + [in_vmem] * 4,
        out_specs=in_vmem,
        scratch_shapes=[
            pltpu.VMEM(pair.shape, jnp.bfloat16),
            pltpu.VMEM((local, gates, ensemble), jnp.float32),
            pltpu.VMEM((local, gates, ensemble), jnp.float32),
            pltpu.VMEM((local, gates, gates), jnp.float32),
            pltpu.VMEM((gates, gates, local), jnp.float32),
            pltpu.VMEM((local, gates, gates), jnp.float32),
            pltpu.VMEM((brick_count, cap * gates + tail, 128), jnp.bfloat16),
            pltpu.VMEM((brick_count, cap * gates, 128), jnp.bfloat16),
            pltpu.VMEM((brick_count, cap * gates + tail, 128), jnp.bfloat16),
            pltpu.VMEM((brick_count, cap * gates, 128), jnp.bfloat16),
            pltpu.VMEM((brick_count, mem_count, out_rows, 128), jnp.bfloat16),
        ]
        + [pltpu.SemaphoreType.DMA((brick_count * PIECES,))] * 2
        + [pltpu.SemaphoreType.DMA((brick_count,))] * 4
        + [pltpu.SemaphoreType.DMA((brick_count * mem_count,))] * 2,
        compiler_params=pltpu.CompilerParams(
            vmem_limit_bytes=48 * 1024 * 1024, collective_id=0, has_side_effects=True
        ),
        cost_estimate=pl.CostEstimate(
            flops=20_000_000_000, bytes_accessed=200_000_000, transcendentals=0
        ),
    )(
        index,
        pair,
        jnp.transpose(observed)[:, :, None],
        jnp.transpose(noise_std)[:, :, None],
        taper_slots,
    ).reshape(devices, out_rows, 128)

    numbers = recv[:, cap * (block + foot) : cap * (block + foot + 1), : foot + 1]
    numbers = numbers.astype(jnp.float32).astype(jnp.int32).reshape(slots, foot + 1)
    filled = numbers[:, foot] == 1
    spots = jnp.arange(slots)
    position = jnp.sum((filled[None, :] & (spots[None, :] < spots[:, None])).astype(jnp.int32), axis=1)
    listed = filled[None, :] & (position[None, :] == spots[:, None])
    slot_list = jnp.sum(jnp.where(listed, spots[None, :], 0), axis=1)
    tile_list = jnp.sum(
        jnp.where(listed[None], jnp.transpose(numbers[:, :foot])[:, None, :], 0), axis=2
    )
    count = jnp.sum(filled.astype(jnp.int32)).reshape(1)

    return pl.pallas_call(
        update_kernel,
        out_shape=jax.ShapeDtypeStruct(members.shape, members.dtype),
        in_specs=[in_smem] * 3 + [in_vmem] * 3,
        out_specs=in_vmem,
        scratch_shapes=[pltpu.VMEM((devices, cap * foot, 128), jnp.float32)],
        compiler_params=vmem,
        cost_estimate=pl.CostEstimate(flops=600_000_000, bytes_accessed=10_000_000, transcendentals=0),
    )(count, slot_list, tile_list, recv, model_all, members)


def solution(mesh):
    in_specs = (
        P("mem", "brick"),
        P("brick", None, "mem"),
        P("brick", None, "mem"),
        P(None, ("mem", "brick")),
        P(None, ("mem", "brick")),
        P(("mem", "brick"), None),
        P(("mem", "brick"), None),
        P(("mem", "brick"), None),
    )
    out_specs = P("mem", "brick")
    return jax.shard_map(body, mesh=mesh, in_specs=in_specs, out_specs=out_specs, check_vma=False)
```

profile of v0, /device:TPU:8, one launch (start us, length us, event | category | flops | bytes accessed | tf_op | source)
XLA Modules:
  0.0 126.8 jit_solution(3435357757113289219)
XLA Ops:
  6.5 0.0 all-gather.2.cloned.1.call-start
  6.6 2.8 %convert_element_type.36 = bf16[32,16384]{1,0:T(8,128)(2,1)} convert(f32[32,16384]{1,0:T(8,128)} %members_ref.1) | non-fusion elementwise | flops 524288 | bytes 3145728 | tf_op jit(solution)/shard_map/convert_element_type | solution.py:294
  9.4 0.0 all-gather.2.cloned.1.call-update
  9.4 0.1 copy.27
  9.5 0.0 copy-done.9
  9.5 0.2 convert_reduce_fusion.1
  9.7 0.0 copy-done.5
  9.7 0.3 convolution_convert_fusion
  10.0 0.1 reshape.71
  10.2 0.0 copy-start.6
  10.2 0.0 copy-start.7
  10.3 1.0 copy.25
  11.3 0.3 copy.20.obs_ref
  11.6 0.0 copy-done.7
  11.6 0.3 copy.21.std_ref
  11.9 0.2 pad.14.clone
  12.1 0.1 select_reduce_fusion.2.index_ref
  12.2 0.0 copy-start
  12.3 79.2 %shard_map.82 = bf16[4,8,304,128]{3,2,1,0:T(8,128)(2,1)S(1)} custom-call(s32[64]{0:T(128)S(1)} %select_reduce_fusion.2.index_ref, bf16[8,32,16,128]{3,2,1,0:T(8,128)(2,1)S(1)} %bitcast.21, f32[32,40,1]{2,1,0:T(8,128)S(1)} %copy.20.obs_ref, f32[32,40,1]{2,1,0:T(8,128)S(1)} %copy.21.std_ref, bf16[8,48,128]{2,1,0:T(8,128)(2,1)S(1)} %fusion.4.taper_ref), custom_call_target="tpu_custom_call" | custom-call | flops 20000000000 | bytes 200000000 | tf_op jit(solution)/shard_map/pallas_call | solution.py:321
  91.5 1.4 %copy-done.1 = bf16[4,8,304,128]{3,2,1,0:T(8,128)(2,1)} copy-done((bf16[4,8,304,128]{3,2,1,0:T(8,128)(2,1)}, bf16[4,8,304,128]{3,2,1,0:T(8,128)(2,1)S(1)}, u32[]{:S(2)}) %copy-start.1) | copy-done | bytes 2490392
  92.9 0.1 slice.23
  93.1 0.1 copy.23
  93.1 0.1 copy.24
  93.2 0.7 convert_reduce_fusion.2
  94.0 0.1 convert_reduce_fusion
  94.1 0.1 select_reduce_fusion.1.slot_ref
  94.2 0.1 fusion.1
  94.3 0.2 select_reduce_fusion.tile_ref
  94.5 0.0 all-gather.2.cloned.1.call-done.model_ref
  94.5 0.0 copy-done
  94.6 1.7 %copy-done.2 = bf16[4,8,304,128]{3,2,1,0:T(8,128)(2,1)S(1)} copy-done((bf16[4,8,304,128]{3,2,1,0:T(8,128)(2,1)S(1)}, bf16[4,8,304,128]{3,2,1,0:T(8,128)(2,1)}, u32[]{:S(2)}) %copy-start.2) | copy-done | bytes 2490392
  96.2 23.7 %shard_map.83 = f32[32,16384]{1,0:T(8,128)} custom-call(s32[1]{0:T(128)} %bitcast.10.count_ref, s32[256]{0:T(256)S(1)} %select_reduce_fusion.1.slot_ref, s32[4,256]{1,0:T(4,128)S(1)} %select_reduce_fusion.tile_ref, bf16[32,304,128]{2,1,0:T(8,128)(2,1)S(1)} %bitcast.20, bf16[128,16384]{1,0:T(8,128)(2,1)} %all-gather.2.cloned.1.call-done.model_ref, ...), custom_call_target="tpu_custom_call" | custom-call | flops 600000000 | bytes 10000000 | tf_op jit(solution)/shard_map/pallas_call | solution.py:368
  (23 shorter events, 0.2 us)
Async XLA Ops:
  6.5 2.9 %copy-start.8 = (s32[32,4]{0,1:T(4,128)S(1)}, s32[32,4]{0,1:T(4,128)}, u32[]{:S(2)}) copy-start(s32[32,4]{0,1:T(4,128)} %param.15) | copy-start | bytes 1540
  6.5 3.0 %copy-start.9 = (s32[32,1]{0,1:T(1,128)S(1)}, s32[32,1]{0,1:T(1,128)}, u32[]{:S(2)}) copy-start(s32[32,1]{0,1:T(1,128)} %param.14) | copy-start | bytes 388
  6.5 3.2 %copy-start.5 = (bf16[32,512]{1,0:T(8,128)(2,1)S(1)}, bf16[32,512]{1,0:T(8,128)(2,1)}, u32[]{:S(2)}) copy-start(bf16[32,512]{1,0:T(8,128)(2,1)} %param.13) | copy-start | bytes 98308
  6.5 3.5 %copy-start.3 = (f32[16,40,256]{2,1,0:T(8,128)S(1)}, f32[16,40,256]{2,1,0:T(8,128)}, u32[]{:S(2)}) copy-start(f32[16,40,256]{2,1,0:T(8,128)} %param.9) | copy-start | bytes 1966084
  6.5 3.6 %copy-start.4 = (f32[16,40,256]{2,1,0:T(8,128)S(1)}, f32[16,40,256]{2,1,0:T(8,128)}, u32[]{:S(2)}) copy-start(f32[16,40,256]{2,1,0:T(8,128)} %param.10) | copy-start | bytes 1966084
  6.5 88.0 %all-gather.2.cloned.1.call-start = ((), (), s32[]{:S(2)}) async-start(), calls=%async_computation | async-start | bytes 5242880 | tf_op jit(solution)/shard_map/all_gather | solution.py:294
  10.2 1.1 copy-start.6
  10.2 1.4 %copy-start.7 = (f32[40,32]{0,1:T(8,128)S(1)}, f32[40,32]{0,1:T(8,128)}, u32[]{:S(2)}) copy-start(f32[40,32]{0,1:T(8,128)} %param.12) | copy-start | bytes 15364
  12.2 82.3 %copy-start = (f32[32,16384]{1,0:T(8,128)S(1)}, f32[32,16384]{1,0:T(8,128)}, u32[]{:S(2)}) copy-start(f32[32,16384]{1,0:T(8,128)} %members_ref.1) | copy-start | bytes 6291460
  91.5 1.5 %copy-start.1 = (bf16[4,8,304,128]{3,2,1,0:T(8,128)(2,1)}, bf16[4,8,304,128]{3,2,1,0:T(8,128)(2,1)S(1)}, u32[]{:S(2)}) copy-start(bf16[4,8,304,128]{3,2,1,0:T(8,128)(2,1)S(1)} %shard_map.82) | copy-start | bytes 7471108
  94.5 1.7 %copy-start.2 = (bf16[4,8,304,128]{3,2,1,0:T(8,128)(2,1)S(1)}, bf16[4,8,304,128]{3,2,1,0:T(8,128)(2,1)}, u32[]{:S(2)}) copy-start(bf16[4,8,304,128]{3,2,1,0:T(8,128)(2,1)} %copy-done.1) | copy-start | bytes 7471108
Sparse Core Ops, SparseCore 0:
  9.5 73.5 all-gather.1
where the time goes:
time: 127 us
  Pallas kernels  103 us (81%)
  between operations  13.6 us (11%)
  local copies, waits for them, and re-layouts  5.44 us (4%)
  other arithmetic  4.47 us (4%)
    pallas_call x1, Pallas kernels, body(): pl.pallas_call(owner_kernel, out_shape=jax.ShapeDtypeStruct((mem_count, b...  79.2 us
    pallas_call x1, Pallas kernels, body(): pl.pallas_call(update_kernel, out_shape=jax.ShapeDtypeStruct(members.shap...  23.7 us
    unnamed x23, local copies, waits for them, and re-layouts  4.39 us
    convert_element_type x1, other arithmetic, body(): members.astype(jnp.bfloat16)  2.77 us
  transfers between devices with their start and end apart: 1, of which 0 were waited for; matrix products, arithmetic and copies ran while one was open for 3% of the time, Pallas kernels for 62%

commit v1 on v0

--- a/solution.py
+++ b/solution.py
@@ -5,7 +5,7 @@
 from jax.experimental.pallas import tpu as pltpu
 from jax.sharding import PartitionSpec as P
 
-GROUP = 4
+GROUP = 8
 PIECES = 4
 HIGH = lax.Precision.HIGHEST
 
@@ -196,20 +196,25 @@
     each_peer(post_gain)
     pack(misf, landed_g, at_b, at_b)
 
+    first = lax.broadcasted_iota(jnp.int32, (2 * gates, ensemble), 0) < gates
+
     def weigh(d):
         source = lax.rem(at_b - d + bricks, bricks)
         for r in range(0, cap, 2):
             gains = landed_g[source, pl.ds(r * gates, 2 * gates), :].astype(jnp.float32)
             anomalies = landed_a[source, pl.ds(r * gates, 2 * gates), :].astype(jnp.float32)
+            sides = jnp.concatenate(
+                [jnp.where(first, anomalies, 0.0), jnp.where(first, 0.0, anomalies)], axis=1
+            )
+            weight = jnp.dot(
+                gains.T.astype(jnp.bfloat16),
+                sides.astype(jnp.bfloat16),
+                preferred_element_type=jnp.float32,
+            ).astype(jnp.bfloat16)
             for h in range(2):
-                weight = jnp.dot(
-                    gains[h * gates : (h + 1) * gates].T.astype(jnp.bfloat16),
-                    anomalies[h * gates : (h + 1) * gates].astype(jnp.bfloat16),
-                    preferred_element_type=jnp.float32,
-                ).astype(jnp.bfloat16)
                 for m in range(mem_count):
                     spread[source, m, pl.ds((r + h) * block, block), :] = weight[
-                        m * block : (m + 1) * block
+                        m * block : (m + 1) * block, h * ensemble : (h + 1) * ensemble
                     ]
         tapers = landed_a[source, pl.ds(held_rows, tail), :]
         for m in range(mem_count):
@@ -260,11 +265,12 @@
             weight = recv_ref[owner, pl.ds(pl.multiple_of(rank * block, block), block), :]
             used = at < total
             starts = [pl.multiple_of(tile_ref[c, at] * 128, 128) for c in range(foot)]
-            cells = jnp.concatenate([model_ref[:, pl.ds(start, 128)] for start in starts], axis=1)
-            part = jnp.dot(weight, cells, preferred_element_type=jnp.float32)
             for c, start in enumerate(starts):
                 taper = tapers[owner, pl.ds(rank * foot + c, 1), :]
-                scaled = part[:, c * 128 : (c + 1) * 128] * taper
+                part = jnp.dot(
+                    weight, model_ref[:, pl.ds(start, 128)], preferred_element_type=jnp.float32
+                )
+                scaled = part * taper
                 results.append((start, jnp.where(used, scaled, 0.0)))
         for start, scaled in results:
             out_ref[:, pl.ds(start, 128)] += scaled

time: 127 us -> 123 us (0.969)
  the two profiles are of different devices: /device:TPU:8 before, /device:TPU:18 now
where the time goes in v1:
time: 123 us
  Pallas kernels  98.8 us (80%)
  between operations  13.6 us (11%)
  local copies, waits for them, and re-layouts  5.44 us (4%)
  other arithmetic  4.47 us (4%)
    pallas_call x1, Pallas kernels, body(): pl.pallas_call(owner_kernel, out_shape=jax.ShapeDtypeStruct((mem_count, b...  80.4 us
    pallas_call x1, Pallas kernels, body(): pl.pallas_call(update_kernel, out_shape=jax.ShapeDtypeStruct(members.shap...  18.4 us
    unnamed x23, local copies, waits for them, and re-layouts  4.39 us
    convert_element_type x1, other arithmetic, body(): members.astype(jnp.bfloat16)  2.77 us
  transfers between devices with their start and end apart: 1, of which 0 were waited for; matrix products, arithmetic and copies ran while one was open for 3% of the time, Pallas kernels for 66%

profile of v1, /device:TPU:18, one launch (start us, length us, event | category | flops | bytes accessed | tf_op | source)
XLA Modules:
  0.0 122.7 jit_solution(16876641255293039231)
XLA Ops:
  6.5 0.0 all-gather.2.cloned.1.call-start
  6.6 2.8 %convert_element_type.36 = bf16[32,16384]{1,0:T(8,128)(2,1)} convert(f32[32,16384]{1,0:T(8,128)} %members_ref.1) | non-fusion elementwise | flops 524288 | bytes 3145728 | tf_op jit(solution)/shard_map/convert_element_type | solution.py:300
  9.4 0.0 all-gather.2.cloned.1.call-update
  9.4 0.0 copy-done.8
  9.4 0.1 copy.27
  9.5 0.0 copy-done.9
  9.5 0.2 convert_reduce_fusion.1
  9.7 0.0 copy-done.5
  9.7 0.3 convolution_convert_fusion
  10.0 0.1 reshape.71
  10.1 0.0 copy-done.4
  10.2 0.0 copy-start.6
  10.2 0.0 copy-start.7
  10.3 1.0 copy.25
  11.3 0.3 copy.20.obs_ref
  11.6 0.3 copy.21.std_ref
  11.9 0.2 pad.14.clone
  12.1 0.1 select_reduce_fusion.2.index_ref
  12.2 0.0 copy-start
  12.3 80.4 %shard_map.82 = bf16[4,8,304,128]{3,2,1,0:T(8,128)(2,1)S(1)} custom-call(s32[64]{0:T(128)S(1)} %select_reduce_fusion.2.index_ref, bf16[8,32,16,128]{3,2,1,0:T(8,128)(2,1)S(1)} %bitcast.21, f32[32,40,1]{2,1,0:T(8,128)S(1)} %copy.20.obs_ref, f32[32,40,1]{2,1,0:T(8,128)S(1)} %copy.21.std_ref, bf16[8,48,128]{2,1,0:T(8,128)(2,1)S(1)} %fusion.4.taper_ref), custom_call_target="tpu_custom_call" | custom-call | flops 20000000000 | bytes 200000000 | tf_op jit(solution)/shard_map/pallas_call | solution.py:327
  92.7 1.4 %copy-done.1 = bf16[4,8,304,128]{3,2,1,0:T(8,128)(2,1)} copy-done((bf16[4,8,304,128]{3,2,1,0:T(8,128)(2,1)}, bf16[4,8,304,128]{3,2,1,0:T(8,128)(2,1)S(1)}, u32[]{:S(2)}) %copy-start.1) | copy-done | bytes 2490392
  94.2 0.1 slice.23
  94.3 0.1 copy.23
  94.4 0.1 copy.24
  94.5 0.7 convert_reduce_fusion.2
  95.2 0.1 convert_reduce_fusion
  95.3 0.1 select_reduce_fusion.1.slot_ref
  95.5 0.1 fusion.1
  95.5 0.2 select_reduce_fusion.tile_ref
  95.8 0.0 all-gather.2.cloned.1.call-done.model_ref
  95.8 1.7 %copy-done.2 = bf16[4,8,304,128]{3,2,1,0:T(8,128)(2,1)S(1)} copy-done((bf16[4,8,304,128]{3,2,1,0:T(8,128)(2,1)S(1)}, bf16[4,8,304,128]{3,2,1,0:T(8,128)(2,1)}, u32[]{:S(2)}) %copy-start.2) | copy-done | bytes 2490392
  97.5 18.4 %shard_map.83 = f32[32,16384]{1,0:T(8,128)} custom-call(s32[1]{0:T(128)} %bitcast.10.count_ref, s32[256]{0:T(256)S(1)} %select_reduce_fusion.1.slot_ref, s32[4,256]{1,0:T(4,128)S(1)} %select_reduce_fusion.tile_ref, bf16[32,304,128]{2,1,0:T(8,128)(2,1)S(1)} %bitcast.20, bf16[128,16384]{1,0:T(8,128)(2,1)} %all-gather.2.cloned.1.call-done.model_ref, ...), custom_call_target="tpu_custom_call" | custom-call | flops 600000000 | bytes 10000000 | tf_op jit(solution)/shard_map/pallas_call | solution.py:374
  (23 shorter events, 0.2 us)
Async XLA Ops:
  6.5 2.9 %copy-start.8 = (s32[32,4]{0,1:T(4,128)S(1)}, s32[32,4]{0,1:T(4,128)}, u32[]{:S(2)}) copy-start(s32[32,4]{0,1:T(4,128)} %param.15) | copy-start | bytes 1540
  6.5 3.0 %copy-start.9 = (s32[32,1]{0,1:T(1,128)S(1)}, s32[32,1]{0,1:T(1,128)}, u32[]{:S(2)}) copy-start(s32[32,1]{0,1:T(1,128)} %param.14) | copy-start | bytes 388
  6.5 3.2 %copy-start.5 = (bf16[32,512]{1,0:T(8,128)(2,1)S(1)}, bf16[32,512]{1,0:T(8,128)(2,1)}, u32[]{:S(2)}) copy-start(bf16[32,512]{1,0:T(8,128)(2,1)} %param.13) | copy-start | bytes 98308
  6.5 3.6 %copy-start.3 = (f32[16,40,256]{2,1,0:T(8,128)S(1)}, f32[16,40,256]{2,1,0:T(8,128)}, u32[]{:S(2)}) copy-start(f32[16,40,256]{2,1,0:T(8,128)} %param.9) | copy-start | bytes 1966084
  6.5 3.6 %copy-start.4 = (f32[16,40,256]{2,1,0:T(8,128)S(1)}, f32[16,40,256]{2,1,0:T(8,128)}, u32[]{:S(2)}) copy-start(f32[16,40,256]{2,1,0:T(8,128)} %param.10) | copy-start | bytes 1966084
  6.5 89.2 %all-gather.2.cloned.1.call-start = ((), (), s32[]{:S(2)}) async-start(), calls=%async_computation | async-start | bytes 5242880 | tf_op jit(solution)/shard_map/all_gather | solution.py:300
  10.2 1.1 copy-start.6
  10.2 1.4 %copy-start.7 = (f32[40,32]{0,1:T(8,128)S(1)}, f32[40,32]{0,1:T(8,128)}, u32[]{:S(2)}) copy-start(f32[40,32]{0,1:T(8,128)} %param.12) | copy-start | bytes 15364
  12.2 83.5 %copy-start = (f32[32,16384]{1,0:T(8,128)S(1)}, f32[32,16384]{1,0:T(8,128)}, u32[]{:S(2)}) copy-start(f32[32,16384]{1,0:T(8,128)} %members_ref.1) | copy-start | bytes 6291460
  92.7 1.5 %copy-start.1 = (bf16[4,8,304,128]{3,2,1,0:T(8,128)(2,1)}, bf16[4,8,304,128]{3,2,1,0:T(8,128)(2,1)S(1)}, u32[]{:S(2)}) copy-start(bf16[4,8,304,128]{3,2,1,0:T(8,128)(2,1)S(1)} %shard_map.82) | copy-start | bytes 7471108
  95.8 1.7 %copy-start.2 = (bf16[4,8,304,128]{3,2,1,0:T(8,128)(2,1)S(1)}, bf16[4,8,304,128]{3,2,1,0:T(8,128)(2,1)}, u32[]{:S(2)}) copy-start(bf16[4,8,304,128]{3,2,1,0:T(8,128)(2,1)} %copy-done.1) | copy-start | bytes 7471108
Sparse Core Ops, SparseCore 0:
  9.5 58.7 all-gather.1
